TPU v7x, 512 devices: a whole 4x4x16 slice. The times are simulated.
512 devices in a mesh: alpha: 32 (over x, y, core), beta: 16 (over z).
Axes of the slice: x: 4, y: 4, z: 16, core: 2. Of those that a mesh axis runs over, the one named last changes fastest.
Arguments:
- vector: float32 [512, 3072], P('alpha', 'beta'), may hold values from -6 to 6
- integrals: float32 [196, 196], replicated, may hold values from -0.078125 to 0.078125
- alpha_targets: int32 [56, 512], replicated, may hold values from 0 to 511
- alpha_pairs: int32 [56, 512], replicated, may hold values from 0 to 195
- alpha_signs: int32 [56, 512], replicated, may hold values from -1 to 1, as said below
- beta_targets: int32 [56, 3072], replicated, may hold values from 0 to 3071
- beta_pairs: int32 [56, 3072], replicated, may hold values from 0 to 195
- beta_signs: int32 [56, 3072], replicated, may hold values from -1 to 1, as said below
Outputs:
- sigma: float32 [512, 3072], P('alpha', 'beta')
Inputs may be any that keep to these rules, and one draw needn't show every extreme that they name: `alpha_signs`: every entry is -1 or 1. `beta_signs`: every entry is -1 or 1.
All inputs are finite; a program needn't handle non-finite values.
Results may differ from a plain program's by a relative error of at most 0.0001.
Values sent between devices are 32-bit elements; how exact they have to be, the bound alone decides.
A program may use at most 64 MiB of HBM per device.

v0:
```python
import math

import jax
import jax.numpy as jnp
from jax import lax
from jax.sharding import PartitionSpec as P


def spin_pass(lookup, targets, pairs, signs, integrals):
    col_count = lookup.shape[0]
    strings = targets.shape[0]
    excite = targets.shape[1]
    pair_count = integrals.shape[0]
    block_size = math.gcd(strings, 128)
    block_count = strings // block_size
    pair_codes = jnp.arange(pair_count, dtype=jnp.int32)

    def one_block(collected, block_lists):
        block_targets, block_pairs, block_signs = block_lists
        flat_targets = block_targets.reshape(-1)
        fetched = jnp.take(lookup, flat_targets, axis=1).reshape(col_count, block_size, excite)
        weights = (block_pairs[..., None] == pair_codes).astype(jnp.float32) * block_signs.astype(
            jnp.float32
        )[..., None]
        density = jnp.einsum("wse,sep->wsp", fetched, weights, precision=lax.Precision.HIGHEST)
        contracted = jnp.einsum("wsp,qp->wsq", density, integrals, precision=lax.Precision.HIGHEST)
        returned = jnp.einsum("wsq,seq->wse", contracted, weights, precision=lax.Precision.HIGHEST)
        collected = collected.at[:, flat_targets].add(
            returned.reshape(col_count, block_size * excite)
        )
        return (collected, None)

    block_lists = (
        targets.reshape(block_count, block_size, excite),
        pairs.reshape(block_count, block_size, excite),
        signs.reshape(block_count, block_size, excite),
    )
    start_value = jnp.zeros((col_count, lookup.shape[1]), jnp.float32)
    collected, _ = lax.scan(one_block, start_value, block_lists)
    return collected


def local(
    vector, integrals, alpha_targets, alpha_pairs, alpha_signs, beta_targets, beta_pairs, beta_signs
):
    alpha_count = vector.shape[0]
    beta_count = vector.shape[1]
    flipped = vector.T
    offset = lax.axis_index("alpha") * alpha_count
    local_lists = [
        lax.dynamic_slice_in_dim(listed, offset, alpha_count, 1).T
        for listed in (alpha_targets, alpha_pairs, alpha_signs)
    ]
    lookup = lax.all_gather(flipped, "alpha", axis=1, tiled=True)
    collected = spin_pass(lookup, local_lists[0], local_lists[1], local_lists[2], integrals)
    alpha_part = lax.psum_scatter(collected, "alpha", scatter_dimension=1, tiled=True).T
    offset = lax.axis_index("beta") * beta_count
    local_lists = [
        lax.dynamic_slice_in_dim(listed, offset, beta_count, 1).T
        for listed in (beta_targets, beta_pairs, beta_signs)
    ]
    lookup = lax.all_gather(vector, "beta", axis=1, tiled=True)
    collected = spin_pass(lookup, local_lists[0], local_lists[1], local_lists[2], integrals)
    beta_part = lax.psum_scatter(collected, "beta", scatter_dimension=1, tiled=True)
    return alpha_part + beta_part


def solution(mesh):
    placed = (P("alpha", "beta"), P(), P(), P(), P(), P(), P(), P())
    return jax.shard_map(
        local, mesh=mesh, in_specs=placed, out_specs=P("alpha", "beta"), check_vma=False
    )
```

profile of v0, /device:TPU:2, one launch (start us, length us, event | category | flops | bytes accessed | tf_op | source)
XLA Modules:
  0.0 356.6 jit_solution(9224061806399364583)
XLA Ops:
  6.5 1.1 copy-done
  7.6 0.1 dynamic-slice_bitcast_fusion.3
  7.7 0.1 copy.37
  7.8 1.0 dynamic-slice_bitcast_fusion.1
  8.9 0.1 copy.38
  9.0 0.1 copy.39
  9.1 37.0 %all-gather = f32[16,192,16]{1,2,0:T(8,128)S(1)} all-gather(f32[1,192,16]{1,2,0:T(8,128)} %bitcast.84), channel_id=1, replica_groups=mesh['alpha'=32,'beta'=16] {'beta'}, dimensions={0}, use_global_device_ids=true | all-gather | bytes 208896 | tf_op jit(solution)/shard_map/all_gather | solution.py:62
  46.1 0.2 copy.40
  46.2 0.1 reshape.170
  46.4 1.6 copy.41
  48.0 0.1 broadcast_in_dim.43
  48.1 0.0 copy-start.3
  48.1 128.9 %while.3 = (s32[]{:T(128)}, f32[16,3072]{0,1:T(8,128)S(1)}, s32[3,64,56]{2,1,0:T(8,128)S(1)}, s32[3,64,56]{2,1,0:T(8,128)S(1)}, s32[3,64,56]{2,1,0:T(8,128)S(1)}...) while((s32[]{:T(128)}, f32[16,3072]{0,1:T(8,128)S(1)}, ...), condition=%wide.region_4.5_spmd.clone, body=%wide.region_2.4_spmd.clone.sunk | while | flops 744766464 | bytes 7072933 | solution.py:39
  48.1 0.1 reshape.197
  48.3 8.7 %gather_fusion = f32[3584,16]{1,0:T(8,128)} fusion(f32[16,3072]{0,1:T(8,128)} %get-tuple-element.198, s32[4096]{0:T(1024)S(1)} %pad_clamp_fusion.3), kind=kCustom, calls=%fused_computation.clone.clone.1 | custom fusion | bytes 473088 | tf_op jit(solution)/shard_map/while/body/eval_jaxpr/jit(_take)/gather | solution.py:21
  57.1 2.0 copy.56
  59.1 3.1 fusion.69
  62.2 1.5 fusion.70
  63.7 4.5 %fusion.71 = f32[16,64,56]{2,0,1:T(8,128)S(1)} fusion(f32[64,56]{1,0:T(8,128)S(1)} %get-tuple-element.174, s32[64,56]{1,0:T(8,128)S(1)} %get-tuple-element.175, f32[16,64,196]{2,1,0:T(8,128)S(1)} %fusion.70), kind=kOutput, calls=%fused_computation.17.clone.1 | convolution fusion | flops 136278016 | bytes 1060864 | tf_op jit(solution)/shard_map/while/body/eval_jaxpr/wsq,seq->wse/dot_general | solution.py:27
  68.3 0.2 copy.57
  68.4 0.3 reshape.198
  68.7 1.8 copy.58
  70.5 20.5 %scatter_fusion = f32[16,3072]{0,1:T(8,128)S(1)} fusion(f32[16,3072]{0,1:T(8,128)S(1)} %get-tuple-element.186, s32[3584]{0:T(1024)S(1)} %fusion.68, f32[3584,16]{1,0:T(8,128)} %copy.58), kind=kCustom, calls=%fused_computation.2.clone.clone.1 | custom fusion | flops 57344 | bytes 702464 | tf_op jit(solution)/shard_map/while/body/eval_jaxpr/scatter-add | solution.py:28
  91.1 0.1 reshape.197
  91.3 8.7 %gather_fusion = f32[3584,16]{1,0:T(8,128)} fusion(f32[16,3072]{0,1:T(8,128)} %get-tuple-element.198, s32[4096]{0:T(1024)S(1)} %pad_clamp_fusion.3), kind=kCustom, calls=%fused_computation.clone.clone.1 | custom fusion | bytes 473088 | tf_op jit(solution)/shard_map/while/body/eval_jaxpr/jit(_take)/gather | solution.py:21
  100.0 2.0 copy.56
  102.0 3.1 fusion.69
  105.2 1.5 fusion.70
  106.7 4.5 %fusion.71 = f32[16,64,56]{2,0,1:T(8,128)S(1)} fusion(f32[64,56]{1,0:T(8,128)S(1)} %get-tuple-element.174, s32[64,56]{1,0:T(8,128)S(1)} %get-tuple-element.175, f32[16,64,196]{2,1,0:T(8,128)S(1)} %fusion.70), kind=kOutput, calls=%fused_computation.17.clone.1 | convolution fusion | flops 136278016 | bytes 1060864 | tf_op jit(solution)/shard_map/while/body/eval_jaxpr/wsq,seq->wse/dot_general | solution.py:27
  111.2 0.2 copy.57
  111.4 0.3 reshape.198
  111.7 1.8 copy.58
  113.5 20.5 %scatter_fusion = f32[16,3072]{0,1:T(8,128)S(1)} fusion(f32[16,3072]{0,1:T(8,128)S(1)} %get-tuple-element.186, s32[3584]{0:T(1024)S(1)} %fusion.68, f32[3584,16]{1,0:T(8,128)} %copy.58), kind=kCustom, calls=%fused_computation.2.clone.clone.1 | custom fusion | flops 57344 | bytes 702464 | tf_op jit(solution)/shard_map/while/body/eval_jaxpr/scatter-add | solution.py:28
  134.1 0.1 reshape.197
  134.2 8.7 %gather_fusion = f32[3584,16]{1,0:T(8,128)} fusion(f32[16,3072]{0,1:T(8,128)} %get-tuple-element.198, s32[4096]{0:T(1024)S(1)} %pad_clamp_fusion.3), kind=kCustom, calls=%fused_computation.clone.clone.1 | custom fusion | bytes 473088 | tf_op jit(solution)/shard_map/while/body/eval_jaxpr/jit(_take)/gather | solution.py:21
  143.0 2.0 copy.56
  145.0 3.1 fusion.69
  148.1 1.5 fusion.70
  149.7 4.5 %fusion.71 = f32[16,64,56]{2,0,1:T(8,128)S(1)} fusion(f32[64,56]{1,0:T(8,128)S(1)} %get-tuple-element.174, s32[64,56]{1,0:T(8,128)S(1)} %get-tuple-element.175, f32[16,64,196]{2,1,0:T(8,128)S(1)} %fusion.70), kind=kOutput, calls=%fused_computation.17.clone.1 | convolution fusion | flops 136278016 | bytes 1060864 | tf_op jit(solution)/shard_map/while/body/eval_jaxpr/wsq,seq->wse/dot_general | solution.py:27
  154.2 0.2 copy.57
  154.3 0.3 reshape.198
  154.6 1.8 copy.58
  156.4 20.5 %scatter_fusion = f32[16,3072]{0,1:T(8,128)S(1)} fusion(f32[16,3072]{0,1:T(8,128)S(1)} %get-tuple-element.186, s32[3584]{0:T(1024)S(1)} %fusion.68, f32[3584,16]{1,0:T(8,128)} %copy.58), kind=kCustom, calls=%fused_computation.2.clone.clone.1 | custom fusion | flops 57344 | bytes 702464 | tf_op jit(solution)/shard_map/while/body/eval_jaxpr/scatter-add | solution.py:28
  177.0 1.1 copy-done.1
  178.1 0.0 reduce-scatter.7.cloned.1.call-update
  178.2 0.0 reduce-scatter.5.cloned.1.call-start
  178.2 0.8 compare_and_fusion.1
  179.0 0.1 copy.33
  179.1 0.1 reshape.132
  179.2 24.8 %all_gather.6 = f32[192,512]{0,1:T(8,128)S(1)} all-gather(f32[192,16]{0,1:T(8,128)S(1)} %bitcast.85), channel_id=1, replica_groups=mesh['alpha'=32,'beta'=16] {'alpha'}, dimensions={1}, use_global_device_ids=true | all-gather | bytes 405504 | tf_op jit(solution)/shard_map/all_gather | solution.py:54
  204.0 0.8 convert_bitcast_fusion.1
  204.9 0.1 copy.35
  204.9 0.1 copy.34
  205.0 0.1 copy.36
  205.1 2.9 gather_fusion.1
  208.0 3.2 fusion.33
  211.2 2.6 fusion.29
  213.8 3.2 fusion.31
  217.0 6.3 %scatter_custom_fusion.1 = f32[192,512]{0,1:T(8,128)} fusion(s32[896]{0:T(1024)S(1)} %fusion.47, f32[896,192]{1,0:T(8,128)S(1)} %bitcast.78, f32[]{:T(128)} %constant.68.clone.1), kind=kCustom, calls=%fused_computation.52 | custom fusion | flops 172032 | bytes 393220 | tf_op jit(solution)/shard_map/while/body/eval_jaxpr/scatter-add | solution.py:28
  223.3 0.0 reduce-scatter.5.cloned.1.call-update
  223.4 22.8 %reduce-scatter.7.cloned.1.call-done = f32[192,16]{1,0:T(8,128)} async-done(((f32[3072,16]{1,0:T(8,128)}), f32[192,16]{1,0:T(8,128)}) %reduce-scatter.7.cloned.1.call-update) | async-done | bytes 12304
  246.2 0.9 copy.44
  247.1 101.3 %reduce-scatter.5.cloned.1.call-done = f32[192,16]{0,1:T(8,128)} async-done(((f32[192,512]{0,1:T(8,128)}), f32[192,16]{0,1:T(8,128)}) %reduce-scatter.5.cloned.1.call-update) | async-done | bytes 12304 | tf_op jit(solution)/shard_map/reduce_scatter | solution.py:56
  348.4 1.3 bitcast_add_fusion
  (20 shorter events, 0.3 us)
Async XLA Ops:
  6.5 1.1 copy-start
  6.5 41.5 %copy-start.2 = (f32[196,196]{1,0:T(8,128)S(1)}, f32[196,196]{1,0:T(8,128)}, u32[]{:S(2)}) copy-start(f32[196,196]{1,0:T(8,128)} %param.11) | copy-start | bytes 460996
  6.5 239.6 %reduce-scatter.7.cloned.1.call-start = ((), (), s32[]{:S(2)}) async-start(), calls=%async_computation.3 | async-start | bytes 1671168
  48.1 131.1 %copy-start.3 = (f32[16,192]{1,0:T(8,128)S(1)}, f32[16,192]{1,0:T(8,128)}, u32[]{:S(2)}) copy-start(f32[16,192]{1,0:T(8,128)} %param.10) | copy-start | bytes 36868
  177.0 1.2 copy-start.1
  178.2 170.3 %reduce-scatter.5.cloned.1.call-start = ((), (), s32[]{:S(2)}) async-start(), calls=%async_computation.2 | async-start | bytes 540672 | tf_op jit(solution)/shard_map/reduce_scatter | solution.py:56
Sparse Core Ops, SparseCore 0:
  178.3 67.8 reduce-scatter.6
  251.1 97.2 reduce-scatter.4
where the time goes:
time: 357 us
  waiting for transfers between devices  124 us (35%)
  other arithmetic  71.2 us (20%)
  blocking collectives  61.8 us (17%)
  local copies, waits for them, and re-layouts  49.1 us (14%)
  matrix products  36.4 us (10%)
  between operations  13.5 us (4%)
    reduce_scatter x1, waiting for transfers between devices, local(): lax.psum_scatter(collected, 'alpha', scatter_dimension=1, tiled=True)  101 us
    scatter-add x4, other arithmetic, one_block(): collected.at[:, flat_targets]  67.9 us
    all_gather x1, blocking collectives, local(): lookup = lax.all_gather(vector, 'beta', axis=1, tiled=True)  37 us
    gather x7, local copies, waits for them, and re-layouts, one_block(): jnp.take(lookup, flat_targets, axis=1)  35.1 us
    all_gather x1, blocking collectives, local(): lookup = lax.all_gather(flipped, 'alpha', axis=1, tiled=True)  24.8 us
    unnamed x3, waiting for transfers between devices  22.8 us
    dot_general x4, matrix products, one_block(): jnp.einsum('wsq,seq->wse', contracted, weights, precision=lax.Precision.H...  16.7 us
    dot_general x4, matrix products, one_block(): jnp.einsum('wse,sep->wsp', fetched, weights, precision=lax.Precision.HIGH...  12.6 us
  transfers between devices with their start and end apart: 2, of which 2 were waited for; matrix products, arithmetic and copies ran while one was open for 6% of the time, Pallas kernels for 0%

commit v1 on v0

v1 whole, which is shorter than its diff:
```python
import functools

import jax
import jax.numpy as jnp
from jax import lax
from jax.experimental import pallas as pl
from jax.experimental.pallas import tpu as pltpu
from jax.sharding import PartitionSpec as P

MESH = pl.DeviceIdType.MESH
F32, BF16, I32 = jnp.float32, jnp.bfloat16, jnp.int32

EXC, PAIRS = 56, 196
NALPHA, NBETA = 32, 16
ROWS, COLS = 16, 192
HIGH, LOW = 12, 256
STEPS, PER_STEP = 12, 8


def dot(a, b):
    return lax.dot_general(a, b, (((1,), (0,)), ((), ())), preferred_element_type=F32)


def dot_t(a, b):
    return lax.dot_general(a, b, (((1,), (1,)), ((), ())), preferred_element_type=F32)


def split(x):
    high = x.astype(BF16)
    return high, (x - high.astype(F32)).astype(BF16)


def iota(shape, dim):
    return lax.broadcasted_iota(I32, shape, dim)


def codes_of(targets, pairs, signs):
    return targets * 512 + pairs * 2 + (signs > 0).astype(I32)


def stack_halves(first, second):
    pad = jnp.zeros((64 - EXC, 128), I32)
    return jnp.concatenate([first, pad, second, pad], axis=0)


def transposed(codes):
    return jnp.transpose(codes.astype(F32)).astype(I32)


def sign_of(codes, entry):
    return jnp.where((entry & 63) < EXC, ((codes & 1) * 2 - 1).astype(F32), 0.0)


def kernel(
    v_ref, m_ref, at_ref, ap_ref, as_ref, bt_ref, bp_ref, bs_ref,
    out_ref,
    alists, blists, list_sem, mpad, mh, ml,
    ga, gz, za, zsplit,
    low_rows, high_rows, pair_rows, sign_rows,
    acol, arow, asum, oh, acc,
    ra_out, ra_in, rz_out, rz_in,
    sa_sem, ga_sem, sz_sem, gz_sem, sra_sem, ra_sem, srz_sem, rz_sem,
):
    a, b = lax.axis_index("alpha"), lax.axis_index("beta")

    def alpha_peer(d):
        return lax.rem(a + d, NALPHA)

    def beta_peer(d):
        return lax.rem(b + d, NBETA)

    def alpha_copy(src, dst, send, recv, d):
        return pltpu.make_async_remote_copy(
            src_ref=src, dst_ref=dst, send_sem=send.at[d], recv_sem=recv.at[d],
            device_id=(alpha_peer(d), b), device_id_type=MESH)

    def beta_copy(src, dst, send, recv, d):
        return pltpu.make_async_remote_copy(
            src_ref=src, dst_ref=dst, send_sem=send.at[d], recv_sem=recv.at[d],
            device_id=(a, beta_peer(d)), device_id_type=MESH)

    awin = pl.multiple_of((a // 8) * 128, 128)
    bwin = pl.multiple_of((b // 2) * 384, 128)
    list_copies = []
    for i, ref in enumerate((at_ref, ap_ref, as_ref)):
        list_copies.append(pltpu.make_async_copy(
            ref.at[:, pl.ds(awin, 128)], alists.at[i], list_sem.at[i]))
    for i, ref in enumerate((bt_ref, bp_ref, bs_ref)):
        list_copies.append(pltpu.make_async_copy(
            ref.at[:, pl.ds(bwin, 384)], blists.at[i], list_sem.at[3 + i]))
    for copy in list_copies:
        copy.start()

    barrier = pltpu.get_barrier_semaphore()

    @pl.loop(1, NALPHA)
    def _(d):
        pl.semaphore_signal(barrier, inc=1, device_id=(alpha_peer(d), b), device_id_type=MESH)

    @pl.loop(1, NBETA)
    def _(d):
        pl.semaphore_signal(barrier, inc=1, device_id=(a, beta_peer(d)), device_id_type=MESH)

    pl.semaphore_wait(barrier, NALPHA + NBETA - 2)

    @pl.loop(1, NBETA)
    def _(d):
        beta_copy(v_ref, gz.at[b], sz_sem, gz_sem, d).start()

    @pl.loop(1, NALPHA)
    def _(d):
        alpha_copy(v_ref, ga.at[a], sa_sem, ga_sem, d).start()

    gz[b] = v_ref[...]
    ga[a] = v_ref[...]
    mpad[...] = jnp.zeros_like(mpad)
    mpad[0:PAIRS, 0:PAIRS] = m_ref[...]
    high, low = split(mpad[...])
    mh[...] = high
    ml[...] = low
    for copy in list_copies:
        copy.wait()

    code = codes_of(alists[0], alists[1], alists[2])
    shift = lax.rem(a, 8) * 16
    first = pltpu.roll(code, lax.rem(128 - shift, 128), 1)
    second = pltpu.roll(code, lax.rem(248 - shift, 128), 1)
    code = stack_halves(first, second)
    acol[...] = code
    arow[...] = transposed(code)

    code = codes_of(blists[0], blists[1], blists[2])
    odd = lax.rem(b, 2) == 1
    first = jnp.where(odd, pltpu.roll(code, 192, 1)[:, :128], code[:, :128])
    second = jnp.where(odd, pltpu.roll(code, 96, 1)[:, :128], pltpu.roll(code, 288, 1)[:, :128])
    code = transposed(stack_halves(first, second))
    sign_rows[...] = sign_of(code, iota((128, 128), 1))
    pair_rows[...] = (code >> 1) & 255
    low_rows[...] = (code >> 9) & 255
    high_rows[...] = code >> 17

    @pl.loop(1, NALPHA)
    def _(d):
        alpha_copy(v_ref, ga.at[a], sa_sem, ga_sem, d).wait_recv()

    vh, vl = split(ga[...].reshape(NALPHA * ROWS, COLS))
    same = (iota((256, 256), 0) >> 6) == (iota((256, 256), 1) >> 6)
    sigma = None
    for g in range(4):
        oh_c, w_c, oh_r, w_r = [], [], [], []
        for k in (2 * g, 2 * g + 1):
            col = acol[:, k:k + 1]
            oh_c.append(jnp.where((col >> 9) == iota((128, 512), 1), 1.0, 0.0).astype(BF16))
            w_c.append(jnp.where(
                ((col >> 1) & 255) == iota((128, 256), 1), sign_of(col, iota((128, 1), 0)), 0.0
            ).astype(BF16))
            row = arow[k:k + 1, :]
            oh_r.append(jnp.where((row >> 9) == iota((512, 128), 0), 1.0, 0.0).astype(BF16))
            w_r.append(jnp.where(
                ((row >> 1) & 255) == iota((256, 128), 0), sign_of(row, iota((1, 128), 1)), 0.0
            ).astype(BF16))
        oh_c, w_c = jnp.concatenate(oh_c, 0), jnp.concatenate(w_c, 0)
        oh_r, w_r = jnp.concatenate(oh_r, 1), jnp.concatenate(w_r, 1)
        fh, fl = dot(oh_c, vh).astype(BF16), dot(oh_c, vl).astype(BF16)
        uh, ul = dot(w_c, mh[...]).astype(BF16), dot(w_c, ml[...]).astype(BF16)
        kh = jnp.where(same, dot(uh, w_r), 0.0).astype(BF16)
        kl = jnp.where(same, dot(ul, w_r), 0.0).astype(BF16)
        rh, rl = split(dot(kh, fh) + dot(kh, fl) + dot(kl, fh))
        part = dot(oh_r, rh) + dot(oh_r, rl)
        if g == 0:
            asum[...] = part
        else:
            asum[...] += part
    ra_out[...] = asum[...].reshape(NALPHA, ROWS, COLS)

    @pl.loop(1, NALPHA)
    def _(d):
        alpha_copy(ra_out.at[alpha_peer(d)], ra_in.at[a], sra_sem, ra_sem, d).start()

    @pl.loop(1, NBETA)
    def _(d):
        beta_copy(v_ref, gz.at[b], sz_sem, gz_sem, d).wait_recv()

    for i in range(NBETA):
        za[:, COLS * i:COLS * (i + 1)] = gz[i]
    for h in range(HIGH):
        high, low = split(za[:, LOW * h:LOW * (h + 1)])
        zsplit[32 * h:32 * h + 16, :] = high
        zsplit[32 * h + 16:32 * h + 32, :] = low
    acc[...] = jnp.zeros_like(acc)

    quarter = iota((1, 256), 1) >> 6

    @pl.loop(0, STEPS)
    def _(step):
        k0 = pl.multiple_of(step * PER_STEP, PER_STEP)
        lows, highs = low_rows[pl.ds(k0, PER_STEP), :], high_rows[pl.ds(k0, PER_STEP), :]
        pairs, signs = pair_rows[pl.ds(k0, PER_STEP), :], sign_rows[pl.ds(k0, PER_STEP), :]

        def row(x, g):
            return jnp.concatenate([x[2 * g:2 * g + 1, :], x[2 * g + 1:2 * g + 2, :]], axis=1)

        wts, d_high, d_low = [], [], []
        for g in range(4):
            one = jnp.where(row(lows, g) == iota((256, 256), 0), 1.0, 0.0).astype(BF16)
            oh[:, 256 * g:256 * (g + 1)] = one
            picked = dot(zsplit[...], one)
            hrow = row(highs, g)
            f = picked[0:32]
            for h in range(1, HIGH):
                f = jnp.where(hrow == h, picked[32 * h:32 * h + 32], f)
            wt = jnp.where(row(pairs, g) == iota((256, 256), 0), row(signs, g), 0.0).astype(BF16)
            wts.append(wt)
            lhs = jnp.concatenate(
                [jnp.where(quarter == j, f, 0.0).astype(BF16) for j in range(4)], axis=0)
            density = dot_t(lhs, wt)
            for j in range(4):
                dh, dl = split(density[32 * j:32 * j + 16] + density[32 * j + 16:32 * j + 32])
                d_high.append(dh)
                d_low.append(dl)
        d_high, d_low = jnp.concatenate(d_high, 0), jnp.concatenate(d_low, 0)
        image = dot_t(d_high, mh[...]) + dot_t(d_low, mh[...]) + dot_t(d_high, ml[...])
        ih, il = split(image)
        lhs = []
        for g in range(4):
            back = dot(jnp.concatenate([ih[64 * g:64 * g + 64], il[64 * g:64 * g + 64]], 0), wts[g])
            back = back[0:64] + back[64:128]
            r = back[0:16]
            for j in range(1, 4):
                r = jnp.where(quarter == j, back[16 * j:16 * j + 16], r)
            rh = r.astype(BF16).astype(F32)
            r2 = jnp.concatenate([rh, r - rh], 0)
            hrow = row(highs, g)
            lhs.append(jnp.concatenate(
                [jnp.where(hrow == h, r2, 0.0).astype(BF16) for h in range(HIGH)], axis=0))
        acc[...] += dot_t(jnp.concatenate(lhs, 1), oh[...])

    for h in range(HIGH):
        za[:, LOW * h:LOW * (h + 1)] = acc[32 * h:32 * h + 16, :] + acc[32 * h + 16:32 * h + 32, :]
    for i in range(NBETA):
        rz_out[i] = za[:, COLS * i:COLS * (i + 1)]

    @pl.loop(1, NBETA)
    def _(d):
        beta_copy(rz_out.at[beta_peer(d)], rz_in.at[b], srz_sem, rz_sem, d).start()

    ra_in[a] = ra_out[a]
    rz_in[b] = rz_out[b]

    @pl.loop(1, NALPHA)
    def _(d):
        alpha_copy(v_ref, ga.at[a], sa_sem, ga_sem, d).wait_send()
        alpha_copy(ra_out.at[alpha_peer(d)], ra_in.at[a], sra_sem, ra_sem, d).wait()

    total = ra_in[0]
    for i in range(1, NALPHA):
        total = total + ra_in[i]

    @pl.loop(1, NBETA)
    def _(d):
        beta_copy(v_ref, gz.at[b], sz_sem, gz_sem, d).wait_send()
        beta_copy(rz_out.at[beta_peer(d)], rz_in.at[b], srz_sem, rz_sem, d).wait()

    for i in range(NBETA):
        total = total + rz_in[i]
    out_ref[...] = total


def local(vector, integrals, *lists):
    vmem = pl.BlockSpec(memory_space=pltpu.VMEM)
    hbm = pl.BlockSpec(memory_space=pl.ANY)
    dma = pltpu.SemaphoreType.DMA
    return pl.pallas_call(
        kernel,
        out_shape=jax.ShapeDtypeStruct((ROWS, COLS), F32),
        in_specs=[vmem, vmem] + [hbm] * 6,
        out_specs=vmem,
        scratch_shapes=[
            pltpu.VMEM((3, EXC, 128), I32),
            pltpu.VMEM((3, EXC, 384), I32),
            dma((6,)),
            pltpu.VMEM((256, 256), F32),
            pltpu.VMEM((256, 256), BF16),
            pltpu.VMEM((256, 256), BF16),
            pltpu.VMEM((NALPHA, ROWS, COLS), F32),
            pltpu.VMEM((NBETA, ROWS, COLS), F32),
            pltpu.VMEM((ROWS, NBETA * COLS), F32),
            pltpu.VMEM((2 * HIGH * ROWS, LOW), BF16),
            pltpu.VMEM((128, 128), I32),
            pltpu.VMEM((128, 128), I32),
            pltpu.VMEM((128, 128), I32),
            pltpu.VMEM((128, 128), F32),
            pltpu.VMEM((128, 128), I32),
            pltpu.VMEM((128, 128), I32),
            pltpu.VMEM((NALPHA * ROWS, COLS), F32),
            pltpu.VMEM((LOW, 1024), BF16),
            pltpu.VMEM((2 * HIGH * ROWS, LOW), F32),
            pltpu.VMEM((NALPHA, ROWS, COLS), F32),
            pltpu.VMEM((NALPHA, ROWS, COLS), F32),
            pltpu.VMEM((NBETA, ROWS, COLS), F32),
            pltpu.VMEM((NBETA, ROWS, COLS), F32),
            dma((NALPHA,)), dma((NALPHA,)), dma((NBETA,)), dma((NBETA,)),
            dma((NALPHA,)), dma((NALPHA,)), dma((NBETA,)), dma((NBETA,)),
        ],
        compiler_params=pltpu.CompilerParams(
            collective_id=0, has_side_effects=True, vmem_limit_bytes=48 * 1024 * 1024),
    )(vector, integrals, *lists)


def solution(mesh):
    placed = (P("alpha", "beta"), P(), P(), P(), P(), P(), P(), P())
    return jax.shard_map(
        local, mesh=mesh, in_specs=placed, out_specs=P("alpha", "beta"), check_vma=False
    )
```

time: 357 us -> 80.2 us (0.22)
  waiting for transfers between devices: 124 us -> 0 us
  Pallas kernels: 0 us -> 71.6 us
  other arithmetic: 71.2 us -> 0 us
  blocking collectives: 61.8 us -> 0 us
  local copies, waits for them, and re-layouts: 49.1 us -> 8.24 us
  matrix products: 36.4 us -> 0 us
  between operations: 13.5 us -> 0.02 us
    reduce_scatter x1 -> x0, waiting for transfers between devices: 101 us -> none  [local(): lax.psum_scatter(collected, 'alpha', scatter_dimension=1, tiled=True)]
    pallas_call x0 -> x1, Pallas kernels: none -> 71.6 us  [local(): pl.pallas_call(kernel, out_shape=jax.ShapeDtypeStruct((ROWS, COLS), F32),...]
    scatter-add x4 -> x0, other arithmetic: 67.9 us -> none  [one_block(): collected.at[:, flat_targets]]
    all_gather x2 -> x0, blocking collectives: 61.8 us -> none  [the longest x1 37 us: local(): lookup = lax.all_gather(vector, 'beta', axis=1, tiled=True)]
    dot_general x12 -> x0, matrix products: 36.4 us -> none  [the longest x4 16.7 us: one_block(): jnp.einsum('wsq,seq->wse', contracted, weights, precision=lax.Precision.H...]
    gather x7 -> x0, local copies, waits for them, and re-layouts: 35.1 us -> none  [one_block(): jnp.take(lookup, flat_targets, axis=1)]
    unnamed x3 -> x0, waiting for transfers between devices: 22.8 us -> none
    reshape x10 -> x0, local copies, waits for them, and re-layouts: 6.64 us -> none  [the longest x6 6.24 us: one_block(): returned.reshape(col_count, block_size * excite)]
  transfers between devices with their start and end apart: 2 -> 0, of which waited for: 2 -> 0; matrix products, arithmetic and copies ran while one was open for 6% -> 0% of each run, Pallas kernels for 0% -> 0%
where the time goes in v1:
time: 80.2 us; the launch traced here: 79.8 us
  Pallas kernels  71.6 us (89%)
  local copies, waits for them, and re-layouts  8.24 us (10%)
    pallas_call x1, Pallas kernels, local(): pl.pallas_call(kernel, out_shape=jax.ShapeDtypeStruct((ROWS, COLS), F32),...  71.6 us
    unnamed x17, local copies, waits for them, and re-layouts  8.24 us

profile of v1, /device:TPU:2, one launch (start us, length us, event | category | flops | bytes accessed | tf_op | source)
XLA Modules:
  0.0 79.8 jit_solution(1810220324641496449)
XLA Ops:
  0.0 0.0 copy-start
  0.0 1.1 %copy-done = s32[56,3072]{1,0:T(8,128)S(1)} copy-done((s32[56,3072]{1,0:T(8,128)S(1)}, s32[56,3072]{1,0:T(8,128)}, u32[]{:S(2)}) %copy-start) | copy-done | bytes 688152
  1.1 0.0 copy-start.1
  1.1 1.1 %copy-done.1 = s32[56,3072]{1,0:T(8,128)S(1)} copy-done((s32[56,3072]{1,0:T(8,128)S(1)}, s32[56,3072]{1,0:T(8,128)}, u32[]{:S(2)}) %copy-start.1) | copy-done | bytes 688152
  2.2 0.0 copy-start.2
  2.2 1.1 %copy-done.2 = s32[56,3072]{1,0:T(8,128)S(1)} copy-done((s32[56,3072]{1,0:T(8,128)S(1)}, s32[56,3072]{1,0:T(8,128)}, u32[]{:S(2)}) %copy-start.2) | copy-done | bytes 688152
  3.3 0.0 copy-start.3
  3.3 0.9 %copy-done.3 = f32[196,196]{1,0:T(8,128)S(1)} copy-done((f32[196,196]{1,0:T(8,128)S(1)}, f32[196,196]{1,0:T(8,128)}, u32[]{:S(2)}) %copy-start.3) | copy-done | bytes 153688
  4.2 0.0 copy-start.4
  4.2 0.9 %copy-done.4 = s32[56,512]{1,0:T(8,128)S(1)} copy-done((s32[56,512]{1,0:T(8,128)S(1)}, s32[56,512]{1,0:T(8,128)}, u32[]{:S(2)}) %copy-start.4) | copy-done | bytes 114712
  5.1 0.0 copy-start.5
  5.1 0.9 %copy-done.5 = s32[56,512]{1,0:T(8,128)S(1)} copy-done((s32[56,512]{1,0:T(8,128)S(1)}, s32[56,512]{1,0:T(8,128)}, u32[]{:S(2)}) %copy-start.5) | copy-done | bytes 114712
  6.0 0.0 copy-start.6
  6.0 0.9 %copy-done.6 = s32[56,512]{1,0:T(8,128)S(1)} copy-done((s32[56,512]{1,0:T(8,128)S(1)}, s32[56,512]{1,0:T(8,128)}, u32[]{:S(2)}) %copy-start.6) | copy-done | bytes 114712
  6.9 0.0 copy-start.7
  6.9 0.7 copy-done.7
  7.6 71.6 %shard_map.82 = f32[16,192]{1,0:T(8,128)S(1)} custom-call(f32[16,192]{1,0:T(8,128)S(1)} %copy-done.7, f32[196,196]{1,0:T(8,128)S(1)} %copy-done.3, s32[56,512]{1,0:T(8,128)S(1)} %copy-done.4, s32[56,512]{1,0:T(8,128)S(1)} %copy-done.5, s32[56,512]{1,0:T(8,128)S(1)} %copy-done.6, s32[56,3072]{1,0:T(8,128)S(1)} %copy-done, s32[56,3072]{1,0:T(8,128)S(1)} %copy-done.1, ...), custom_call_target="tpu_custom_call" | custom-call | tf_op jit(solution)/shard_map/pallas_call | solution.py:273
  79.2 0.6 copy.10
Async XLA Ops:
  0.0 1.1 %copy-start = (s32[56,3072]{1,0:T(8,128)S(1)}, s32[56,3072]{1,0:T(8,128)}, u32[]{:S(2)}) copy-start(s32[56,3072]{1,0:T(8,128)} %bt_ref.1) | copy-start | bytes 2064388
  1.1 1.1 %copy-start.1 = (s32[56,3072]{1,0:T(8,128)S(1)}, s32[56,3072]{1,0:T(8,128)}, u32[]{:S(2)}) copy-start(s32[56,3072]{1,0:T(8,128)} %bp_ref.1) | copy-start | bytes 2064388
  2.2 1.1 %copy-start.2 = (s32[56,3072]{1,0:T(8,128)S(1)}, s32[56,3072]{1,0:T(8,128)}, u32[]{:S(2)}) copy-start(s32[56,3072]{1,0:T(8,128)} %bs_ref.1) | copy-start | bytes 2064388
  3.3 0.9 %copy-start.3 = (f32[196,196]{1,0:T(8,128)S(1)}, f32[196,196]{1,0:T(8,128)}, u32[]{:S(2)}) copy-start(f32[196,196]{1,0:T(8,128)} %m_ref.1) | copy-start | bytes 460996
  4.2 0.9 %copy-start.4 = (s32[56,512]{1,0:T(8,128)S(1)}, s32[56,512]{1,0:T(8,128)}, u32[]{:S(2)}) copy-start(s32[56,512]{1,0:T(8,128)} %at_ref.1) | copy-start | bytes 344068
  5.1 0.9 %copy-start.5 = (s32[56,512]{1,0:T(8,128)S(1)}, s32[56,512]{1,0:T(8,128)}, u32[]{:S(2)}) copy-start(s32[56,512]{1,0:T(8,128)} %ap_ref.1) | copy-start | bytes 344068
  6.0 0.9 %copy-start.6 = (s32[56,512]{1,0:T(8,128)S(1)}, s32[56,512]{1,0:T(8,128)}, u32[]{:S(2)}) copy-start(s32[56,512]{1,0:T(8,128)} %as_ref.1) | copy-start | bytes 344068
  6.9 0.7 copy-start.7

commit v2 on v1

v2 whole, which is shorter than its diff:
```python
import jax
import jax.numpy as jnp
from jax import lax
from jax.experimental import pallas as pl
from jax.experimental.pallas import tpu as pltpu
from jax.sharding import PartitionSpec as P

MESH = pl.DeviceIdType.MESH
F32, BF16, I32 = jnp.float32, jnp.bfloat16, jnp.int32

EXC, PAIRS = 56, 196
NALPHA, NBETA = 32, 16
ROWS, COLS = 16, 192
HIGH, LOW = 12, 256
STEPS = 12
TILES = 4 * STEPS
ENTRIES = 256 * TILES


def dot(a, b):
    return lax.dot_general(a, b, (((1,), (0,)), ((), ())), preferred_element_type=F32)


def dot_t(a, b):
    return lax.dot_general(a, b, (((1,), (1,)), ((), ())), preferred_element_type=F32)


def split(x):
    high = x.astype(BF16)
    return high, (x - high.astype(F32)).astype(BF16)


def iota(shape, dim):
    return lax.broadcasted_iota(I32, shape, dim)


def codes_of(targets, pairs, signs):
    return targets * 512 + pairs * 2 + (signs > 0).astype(I32)


def stack_halves(first, second):
    pad = jnp.zeros((64 - EXC, 128), I32)
    return jnp.concatenate([first, pad, second, pad], axis=0)


def transposed(codes):
    return jnp.transpose(codes.astype(F32)).astype(I32)


def sign_of(codes, entry):
    return jnp.where((entry & 63) < EXC, ((codes & 1) * 2 - 1).astype(F32), 0.0)


def pair_of(codes):
    return (codes >> 1) & 255


def low_of(codes):
    return (codes >> 9) & 255


def one_hot(index, width, value=1.0):
    if index.shape[1] == 1:
        where = iota((index.shape[0], width), 1)
    else:
        where = iota((width, index.shape[1]), 0)
    return jnp.where(index == where, value, 0.0).astype(BF16)


def kernel(
    v_hbm, m_hbm, at_ref, ap_ref, as_ref, bt_ref, bp_ref, bs_ref,
    out_ref,
    v_ref, m_ref, alists, blists, list_sem, mpad, mh, ml,
    ga, gz, za, zsplit,
    acol, arow, a_oh_c, a_oh_r, a_kh, a_kl, asum,
    bcol, brow, b_oh_c, b_oh_r, b_k, fetched, returned, acc,
    ra_out, ra_in, rz_out, rz_in, rz_sum, rz_far,
    sa_sem, ga_sem, sz_sem, gz_sem, sra_sem, ra_sem, srz_sem, rz_sem,
):
    a, b = lax.axis_index("alpha"), lax.axis_index("beta")

    def alpha_peer(d):
        return lax.rem(a + d, NALPHA)

    def beta_peer(d):
        return lax.rem(b + d + NBETA, NBETA)

    def alpha_copy(src, dst, send, recv, d):
        return pltpu.make_async_remote_copy(
            src_ref=src, dst_ref=dst, send_sem=send.at[d], recv_sem=recv.at[d],
            device_id=(alpha_peer(d), b), device_id_type=MESH)

    def beta_copy(src, dst, send, recv, n, d):
        return pltpu.make_async_remote_copy(
            src_ref=src, dst_ref=dst, send_sem=send.at[n], recv_sem=recv.at[n],
            device_id=(a, beta_peer(d)), device_id_type=MESH)

    barrier = pltpu.get_barrier_semaphore()
    near = (4, -4, 1, -1, 2, -2)
    for d in near:
        pl.semaphore_signal(barrier, inc=1, device_id=(a, beta_peer(d)), device_id_type=MESH)

    @pl.loop(1, NALPHA)
    def _(d):
        pl.semaphore_signal(barrier, inc=1, device_id=(alpha_peer(d), b), device_id_type=MESH)

    awin = pl.multiple_of((a // 8) * 128, 128)
    bwin = pl.multiple_of((b // 2) * 384, 128)
    copies = [
        pltpu.make_async_copy(v_hbm, v_ref, list_sem.at[6]),
        pltpu.make_async_copy(m_hbm, m_ref, list_sem.at[7]),
    ]
    for i, ref in enumerate((at_ref, ap_ref, as_ref)):
        copies.append(pltpu.make_async_copy(
            ref.at[:, pl.ds(awin, 128)], alists.at[i], list_sem.at[i]))
    for i, ref in enumerate((bt_ref, bp_ref, bs_ref)):
        copies.append(pltpu.make_async_copy(
            ref.at[:, pl.ds(bwin, 384)], blists.at[i], list_sem.at[3 + i]))
    for copy in copies:
        copy.start()
    for copy in copies:
        copy.wait()

    gz[b] = v_ref[...]
    ga[a] = v_ref[...]
    mpad[...] = jnp.zeros_like(mpad)
    mpad[0:PAIRS, 0:PAIRS] = m_ref[...]
    high, low = split(mpad[...])
    mh[...] = high
    ml[...] = low

    code = codes_of(blists[0], blists[1], blists[2])
    odd = lax.rem(b, 2) == 1
    first = jnp.where(odd, pltpu.roll(code, 192, 1)[:, :128], code[:, :128])
    second = jnp.where(odd, pltpu.roll(code, 96, 1)[:, :128], pltpu.roll(code, 288, 1)[:, :128])
    code = stack_halves(first, second)
    bcol[...] = code
    brow[...] = transposed(code)

    code = codes_of(alists[0], alists[1], alists[2])
    shift = lax.rem(a, 8) * 16
    first = pltpu.roll(code, lax.rem(128 - shift, 128), 1)
    second = pltpu.roll(code, lax.rem(248 - shift, 128), 1)
    code = stack_halves(first, second)
    acol[...] = code
    arow[...] = transposed(code)

    pl.semaphore_wait(barrier, NALPHA - 1 + len(near))

    def z_first():
        return [beta_copy(v_ref, gz.at[b], sz_sem, gz_sem, n, d) for n, d in enumerate(near)]

    def z_second():
        up, down = beta_peer(4), beta_peer(-4)
        top, bottom = pl.ds(0, 8), pl.ds(8, 8)
        return [
            beta_copy(gz.at[down, top], gz.at[down, top], sz_sem, gz_sem, 6, 4),
            beta_copy(gz.at[up, bottom], gz.at[up, bottom], sz_sem, gz_sem, 7, -4),
            beta_copy(gz.at[up], gz.at[up], sz_sem, gz_sem, 8, 1),
            beta_copy(gz.at[up], gz.at[up], sz_sem, gz_sem, 9, -1),
            beta_copy(gz.at[down], gz.at[down], sz_sem, gz_sem, 10, 1),
            beta_copy(gz.at[down], gz.at[down], sz_sem, gz_sem, 11, -1),
            beta_copy(gz.at[down], gz.at[down], sz_sem, gz_sem, 12, 2),
            beta_copy(gz.at[up], gz.at[up], sz_sem, gz_sem, 13, -2),
        ]

    def z_third():
        far = beta_peer(8)
        return [
            beta_copy(gz.at[far], gz.at[far], sz_sem, gz_sem, 14, 1),
            beta_copy(gz.at[far], gz.at[far], sz_sem, gz_sem, 15, -1),
        ]

    for copy in z_first():
        copy.start()

    @pl.loop(1, NALPHA)
    def _(d):
        alpha_copy(v_ref, ga.at[a], sa_sem, ga_sem, d).start()

    left_half = iota((1, 128), 1) < 64

    def beta_step(step):
        rows = brow[pl.ds(pl.multiple_of(step * 8, 8), 8), :]
        cols = pltpu.roll(bcol[...], lax.rem(128 - 8 * step, 128), 1)
        w_c, w_r = [], []
        for k in range(8):
            at = pl.multiple_of(step * 1024 + 128 * k, 128)
            col = cols[:, k:k + 1]
            b_oh_c[pl.ds(at, 128), :] = one_hot(low_of(col), LOW)
            w_c.append(one_hot(pair_of(col), 256, sign_of(col, iota((128, 1), 0))))
            row = rows[k:k + 1, :]
            b_oh_r[:, pl.ds(at, 128)] = one_hot(low_of(row), LOW)
            w_r.append(one_hot(pair_of(row), 256, sign_of(row, iota((1, 128), 1))))
        w_c = jnp.concatenate(w_c, 0)
        uh, ul = dot_t(w_c, mh[...]).astype(BF16), dot_t(w_c, ml[...]).astype(BF16)
        for g in range(4):
            w = jnp.concatenate([w_r[2 * g], w_r[2 * g + 1]], 1)
            kh = dot(uh[256 * g:256 * g + 256], w)
            kl = dot(ul[256 * g:256 * g + 256], w)
            for j in range(4):
                sl = slice(64 * j, 64 * j + 64), slice(128 * (j // 2), 128 * (j // 2) + 128)
                one, two = kh[sl], pltpu.roll(kl[sl], 64, 1)
                mine = left_half if j % 2 == 0 else ~left_half
                b_k[step * 4 + g, 64 * j:64 * j + 64, :] = jnp.where(mine, one, two).astype(BF16)

    same = (iota((256, 256), 0) >> 6) == (iota((256, 256), 1) >> 6)

    def alpha_prepare():
        for g in range(4):
            w_c, w_r = [], []
            for k in (2 * g, 2 * g + 1):
                col, row = acol[:, k:k + 1], arow[k:k + 1, :]
                a_oh_c[128 * k:128 * k + 128, :] = one_hot(col >> 9, NALPHA * ROWS)
                a_oh_r[:, 128 * k:128 * k + 128] = one_hot(row >> 9, NALPHA * ROWS)
                w_c.append(one_hot(pair_of(col), 256, sign_of(col, iota((128, 1), 0))))
                w_r.append(one_hot(pair_of(row), 256, sign_of(row, iota((1, 128), 1))))
            w_c, w_r = jnp.concatenate(w_c, 0), jnp.concatenate(w_r, 1)
            uh, ul = dot(w_c, mh[...]).astype(BF16), dot(w_c, ml[...]).astype(BF16)
            a_kh[g] = jnp.where(same, dot(uh, w_r), 0.0).astype(BF16)
            a_kl[g] = jnp.where(same, dot(ul, w_r), 0.0).astype(BF16)

    pl.loop(0, 4)(beta_step)
    for copy in z_first():
        copy.wait_recv()
    for copy in z_second():
        copy.start()
    pl.loop(4, 8)(beta_step)
    for copy in z_second():
        copy.wait_recv()
    for copy in z_third():
        copy.start()
    alpha_prepare()
    pl.loop(8, STEPS)(beta_step)

    @pl.loop(1, NALPHA)
    def _(d):
        alpha_copy(v_ref, ga.at[a], sa_sem, ga_sem, d).wait_recv()

    vh, vl = split(ga[...].reshape(NALPHA * ROWS, COLS))
    fh, fl = dot(a_oh_c[...], vh).astype(BF16), dot(a_oh_c[...], vl).astype(BF16)
    rh, rl = [], []
    for g in range(4):
        mine = slice(256 * g, 256 * g + 256)
        high, low = split(
            dot(a_kh[g], fh[mine]) + dot(a_kh[g], fl[mine]) + dot(a_kl[g], fh[mine]))
        rh.append(high)
        rl.append(low)
    rh, rl = jnp.concatenate(rh, 0), jnp.concatenate(rl, 0)
    asum = dot(a_oh_r[...], rh) + dot(a_oh_r[...], rl)
    ra_out[...] = asum.reshape(NALPHA, ROWS, COLS)

    @pl.loop(1, NALPHA)
    def _(d):
        alpha_copy(ra_out.at[alpha_peer(d)], ra_in.at[a], sra_sem, ra_sem, d).start()

    for copy in z_third():
        copy.wait_recv()
    for i in range(NBETA):
        za[:, COLS * i:COLS * (i + 1)] = gz[i]
    for h in range(HIGH):
        high, low = split(za[:, LOW * h:LOW * (h + 1)])
        zsplit[32 * h:32 * h + 16, :] = high
        zsplit[32 * h + 16:32 * h + 32, :] = low
    acc[...] = jnp.zeros_like(acc)

    quarter = iota((1, 256), 1) >> 6

    def high_rows(step):
        return brow[pl.ds(pl.multiple_of(step * 8, 8), 8), :] >> 17

    def pair_row(rows, g):
        return jnp.concatenate([rows[2 * g:2 * g + 1, :], rows[2 * g + 1:2 * g + 2, :]], axis=1)

    @pl.loop(0, STEPS)
    def _(step):
        highs = high_rows(step)
        for g in range(4):
            at = pl.multiple_of(step * 1024 + 256 * g, 256)
            picked = dot(zsplit[...], b_oh_r[:, pl.ds(at, 256)])
            hrow = pair_row(highs, g)
            f = picked[0:32]
            for h in range(1, HIGH):
                f = jnp.where(hrow == h, picked[32 * h:32 * h + 32], f)
            fetched[:, pl.ds(at, 256)] = f.astype(BF16)

    @pl.loop(0, STEPS)
    def _(step):
        for g in range(4):
            at = pl.multiple_of(step * 1024 + 256 * g, 256)
            f = fetched[:, pl.ds(at, 256)].astype(F32)
            lhs = jnp.concatenate(
                [jnp.where(quarter == j, f, 0.0).astype(BF16) for j in range(4)], axis=0)
            back = dot(lhs, b_k[step * 4 + g])
            parts = []
            for j in (0, 2):
                h0, l0 = back[32 * j:32 * j + 16], back[32 * j + 16:32 * j + 32]
                h1, l1 = back[32 * j + 32:32 * j + 48], back[32 * j + 48:32 * j + 64]
                parts.append(jnp.where(left_half, h0 + l0, h1 + l1)
                             + pltpu.roll(jnp.where(left_half, h1, h0), 64, 1))
            r = jnp.concatenate(parts, 1)
            high, low = split(r)
            returned[0:16, pl.ds(at, 256)] = high
            returned[16:32, pl.ds(at, 256)] = low

    @pl.loop(0, STEPS)
    def _(step):
        highs = high_rows(step)
        lhs = []
        for g in range(4):
            at = pl.multiple_of(step * 1024 + 256 * g, 256)
            r = returned[:, pl.ds(at, 256)].astype(F32)
            hrow = pair_row(highs, g)
            lhs.append(jnp.concatenate(
                [jnp.where(hrow == h, r, 0.0).astype(BF16) for h in range(HIGH)], axis=0))
        at = pl.multiple_of(step * 1024, 1024)
        acc[...] += dot(jnp.concatenate(lhs, 1), b_oh_c[pl.ds(at, 1024), :])

    for h in range(HIGH):
        za[:, LOW * h:LOW * (h + 1)] = acc[32 * h:32 * h + 16, :] + acc[32 * h + 16:32 * h + 32, :]
    for i in range(NBETA):
        rz_out[i] = za[:, COLS * i:COLS * (i + 1)]

    def near_copies():
        made = []
        for n, (d, k) in enumerate(((1, 2), (-1, 2), (1, 1), (-1, 1), (1, 3), (-1, 3), (2, 1),
                                    (-2, 3), (1, 0), (-1, 0), (2, 0), (-2, 0))):
            made.append(beta_copy(rz_out.at[beta_peer(d + 4 * k)], rz_in.at[n], srz_sem, rz_sem, n, d))
        return made

    made = near_copies()
    for copy in made:
        copy.start()
    top, bottom = pl.ds(0, 8), pl.ds(8, 8)
    far = [
        beta_copy(rz_sum.at[2, top], rz_far.at[0, top], srz_sem, rz_sem, 12, 4),
        beta_copy(rz_sum.at[2, bottom], rz_far.at[0, bottom], srz_sem, rz_sem, 13, -4),
        beta_copy(rz_sum.at[1], rz_far.at[1], srz_sem, rz_sem, 14, 4),
        beta_copy(rz_sum.at[3], rz_far.at[2], srz_sem, rz_sem, 15, -4),
    ]
    made[0].wait_recv()
    made[1].wait_recv()
    rz_sum[2] = rz_out[beta_peer(8)] + rz_in[0] + rz_in[1]
    far[0].start()
    far[1].start()
    for n in range(2, 12):
        made[n].wait_recv()
    s1 = rz_out[beta_peer(4)] + rz_in[2] + rz_in[3] + rz_in[6]
    s3 = rz_out[beta_peer(12)] + rz_in[4] + rz_in[5] + rz_in[7]
    total = rz_out[b] + rz_in[8] + rz_in[9] + rz_in[10] + rz_in[11]
    far[0].wait_recv()
    far[1].wait_recv()
    rz_sum[1, 0:8] = s1[0:8] + rz_far[0, 0:8]
    rz_sum[1, 8:16] = s1[8:16]
    rz_sum[3, 0:8] = s3[0:8]
    rz_sum[3, 8:16] = s3[8:16] + rz_far[0, 8:16]
    far[2].start()
    far[3].start()

    total = total + ra_out[a]

    @pl.loop(1, NALPHA)
    def _(d):
        alpha_copy(v_ref, ga.at[a], sa_sem, ga_sem, d).wait_send()
        alpha_copy(ra_out.at[alpha_peer(d)], ra_in.at[a], sra_sem, ra_sem, d).wait()

    ra_in[a] = jnp.zeros((ROWS, COLS), F32)
    for i in range(NALPHA):
        total = total + ra_in[i]
    for copy in z_first() + z_second() + z_third() + made + far:
        copy.wait_send()
    far[2].wait_recv()
    far[3].wait_recv()
    out_ref[...] = total + rz_far[1] + rz_far[2]


def local(vector, integrals, *lists):
    vmem = pl.BlockSpec(memory_space=pltpu.VMEM)
    hbm = pl.BlockSpec(memory_space=pltpu.HBM)
    dma = pltpu.SemaphoreType.DMA

    def block(*shape):
        return pltpu.VMEM(shape, F32)

    return pl.pallas_call(
        kernel,
        out_shape=jax.ShapeDtypeStruct((ROWS, COLS), F32),
        in_specs=[hbm] * 8,
        out_specs=vmem,
        scratch_shapes=[
            block(ROWS, COLS),
            block(PAIRS, PAIRS),
            pltpu.VMEM((3, EXC, 128), I32),
            pltpu.VMEM((3, EXC, 384), I32),
            dma((8,)),
            block(256, 256),
            pltpu.VMEM((256, 256), BF16),
            pltpu.VMEM((256, 256), BF16),
            block(NALPHA, ROWS, COLS),
            block(NBETA, ROWS, COLS),
            block(ROWS, NBETA * COLS),
            pltpu.VMEM((2 * HIGH * ROWS, LOW), BF16),
            pltpu.VMEM((128, 128), I32),
            pltpu.VMEM((128, 128), I32),
            pltpu.VMEM((1024, NALPHA * ROWS), BF16),
            pltpu.VMEM((NALPHA * ROWS, 1024), BF16),
            pltpu.VMEM((4, 256, 256), BF16),
            pltpu.VMEM((4, 256, 256), BF16),
            block(NALPHA * ROWS, COLS),
            pltpu.VMEM((128, 128), I32),
            pltpu.VMEM((128, 128), I32),
            pltpu.VMEM((ENTRIES, LOW), BF16),
            pltpu.VMEM((LOW, ENTRIES), BF16),
            pltpu.VMEM((TILES, 256, 128), BF16),
            pltpu.VMEM((2 * ROWS, ENTRIES), BF16),
            pltpu.VMEM((2 * ROWS, ENTRIES), BF16),
            block(2 * HIGH * ROWS, LOW),
            block(NALPHA, ROWS, COLS),
            block(NALPHA, ROWS, COLS),
            block(NBETA, ROWS, COLS),
            block(12, ROWS, COLS),
            block(4, ROWS, COLS),
            block(3, ROWS, COLS),
            dma((NALPHA,)), dma((NALPHA,)), dma((NBETA,)), dma((NBETA,)),
            dma((NALPHA,)), dma((NALPHA,)), dma((NBETA,)), dma((NBETA,)),
        ],
        compiler_params=pltpu.CompilerParams(
            collective_id=0, has_side_effects=True, vmem_limit_bytes=52 * 1024 * 1024),
    )(vector, integrals, *lists)


def solution(mesh):
    placed = (P("alpha", "beta"), P(), P(), P(), P(), P(), P(), P())
    return jax.shard_map(
        local, mesh=mesh, in_specs=placed, out_specs=P("alpha", "beta"), check_vma=False
    )
```

time: 80.2 us -> 68.5 us (0.85)
  Pallas kernels: 71.6 us -> 61 us
  local copies, waits for them, and re-layouts: 8.24 us -> 7.14 us
    pallas_call x1, Pallas kernels: 71.6 us -> 61 us  [local(): pl.pallas_call(kernel, out_shape=jax.ShapeDtypeStruct((ROWS, COLS), F32),...]
    unnamed x17 -> x15, local copies, waits for them, and re-layouts: 8.24 us -> 7.14 us
where the time goes in v2:
time: 68.5 us; the launch traced here: 68.1 us
  Pallas kernels  61 us (89%)
  local copies, waits for them, and re-layouts  7.14 us (10%)
    pallas_call x1, Pallas kernels, local(): pl.pallas_call(kernel, out_shape=jax.ShapeDtypeStruct((ROWS, COLS), F32),...  61 us
    unnamed x15, local copies, waits for them, and re-layouts  7.14 us

profile of v2, /device:TPU:2, one launch (start us, length us, event | category | flops | bytes accessed | tf_op | source)
XLA Modules:
  0.0 68.1 jit_solution(12479806339028071953)
XLA Ops:
  0.0 0.0 copy-start
  0.0 1.1 %copy-done = s32[56,3072]{1,0:T(8,128)S(1)} copy-done((s32[56,3072]{1,0:T(8,128)S(1)}, s32[56,3072]{1,0:T(8,128)}, u32[]{:S(2)}) %copy-start) | copy-done | bytes 688152
  1.1 0.0 copy-start.1
  1.1 1.1 %copy-done.1 = s32[56,3072]{1,0:T(8,128)S(1)} copy-done((s32[56,3072]{1,0:T(8,128)S(1)}, s32[56,3072]{1,0:T(8,128)}, u32[]{:S(2)}) %copy-start.1) | copy-done | bytes 688152
  2.2 0.0 copy-start.2
  2.2 0.9 %copy-done.2 = f32[196,196]{1,0:T(8,128)S(1)} copy-done((f32[196,196]{1,0:T(8,128)S(1)}, f32[196,196]{1,0:T(8,128)}, u32[]{:S(2)}) %copy-start.2) | copy-done | bytes 153688
  3.1 0.0 copy-start.3
  3.1 0.9 %copy-done.3 = s32[56,512]{1,0:T(8,128)S(1)} copy-done((s32[56,512]{1,0:T(8,128)S(1)}, s32[56,512]{1,0:T(8,128)}, u32[]{:S(2)}) %copy-start.3) | copy-done | bytes 114712
  4.0 0.0 copy-start.4
  4.0 0.9 %copy-done.4 = s32[56,512]{1,0:T(8,128)S(1)} copy-done((s32[56,512]{1,0:T(8,128)S(1)}, s32[56,512]{1,0:T(8,128)}, u32[]{:S(2)}) %copy-start.4) | copy-done | bytes 114712
  4.9 0.0 copy-start.5
  4.9 0.9 %copy-done.5 = s32[56,512]{1,0:T(8,128)S(1)} copy-done((s32[56,512]{1,0:T(8,128)S(1)}, s32[56,512]{1,0:T(8,128)}, u32[]{:S(2)}) %copy-start.5) | copy-done | bytes 114712
  5.8 0.0 copy-start.6
  5.8 0.7 %copy-done.6 = f32[16,192]{1,0:T(8,128)S(1)} copy-done((f32[16,192]{1,0:T(8,128)S(1)}, f32[16,192]{1,0:T(8,128)}, u32[]{:S(2)}) %copy-start.6) | copy-done | bytes 12312
  6.5 61.0 %shard_map.82 = f32[16,192]{1,0:T(8,128)S(1)} custom-call(f32[16,192]{1,0:T(8,128)S(1)} %copy-done.6, f32[196,196]{1,0:T(8,128)S(1)} %copy-done.2, s32[56,512]{1,0:T(8,128)S(1)} %copy-done.3, s32[56,512]{1,0:T(8,128)S(1)} %copy-done.4, s32[56,512]{1,0:T(8,128)S(1)} %copy-done.5, s32[56,3072]{1,0:T(8,128)S(1)} %copy-done, s32[56,3072]{1,0:T(8,128)S(1)} %copy-done.1, ...), custom_call_target="tpu_custom_call" | custom-call | tf_op jit(solution)/shard_map/pallas_call | solution.py:385
  67.5 0.6 copy.10
Async XLA Ops:
  0.0 1.1 %copy-start = (s32[56,3072]{1,0:T(8,128)S(1)}, s32[56,3072]{1,0:T(8,128)}, u32[]{:S(2)}) copy-start(s32[56,3072]{1,0:T(8,128)} %bt_ref.1) | copy-start | bytes 2064388
  1.1 1.1 %copy-start.1 = (s32[56,3072]{1,0:T(8,128)S(1)}, s32[56,3072]{1,0:T(8,128)}, u32[]{:S(2)}) copy-start(s32[56,3072]{1,0:T(8,128)} %bp_ref.1) | copy-start | bytes 2064388
  2.2 0.9 %copy-start.2 = (f32[196,196]{1,0:T(8,128)S(1)}, f32[196,196]{1,0:T(8,128)}, u32[]{:S(2)}) copy-start(f32[196,196]{1,0:T(8,128)} %m_hbm.1) | copy-start | bytes 460996
  3.1 0.9 %copy-start.3 = (s32[56,512]{1,0:T(8,128)S(1)}, s32[56,512]{1,0:T(8,128)}, u32[]{:S(2)}) copy-start(s32[56,512]{1,0:T(8,128)} %at_ref.1) | copy-start | bytes 344068
  4.0 0.9 %copy-start.4 = (s32[56,512]{1,0:T(8,128)S(1)}, s32[56,512]{1,0:T(8,128)}, u32[]{:S(2)}) copy-start(s32[56,512]{1,0:T(8,128)} %ap_ref.1) | copy-start | bytes 344068
  4.9 0.9 %copy-start.5 = (s32[56,512]{1,0:T(8,128)S(1)}, s32[56,512]{1,0:T(8,128)}, u32[]{:S(2)}) copy-start(s32[56,512]{1,0:T(8,128)} %as_ref.1) | copy-start | bytes 344068
  5.8 0.7 %copy-start.6 = (f32[16,192]{1,0:T(8,128)S(1)}, f32[16,192]{1,0:T(8,128)}, u32[]{:S(2)}) copy-start(f32[16,192]{1,0:T(8,128)} %v_hbm.1) | copy-start | bytes 36868

commit v3 on v2

v3 whole, which is shorter than its diff:
```python
import jax
import jax.numpy as jnp
from jax import lax
from jax.experimental import pallas as pl
from jax.experimental.pallas import tpu as pltpu
from jax.sharding import PartitionSpec as P

MESH = pl.DeviceIdType.MESH
F32, BF16, I32 = jnp.float32, jnp.bfloat16, jnp.int32

EXC, PAIRS = 56, 196
NALPHA, NBETA = 32, 16
ROWS, COLS = 16, 192
HIGH, LOW = 12, 256
STEPS = 12
TILES = 4 * STEPS
ENTRIES = 256 * TILES


def dot(a, b):
    return lax.dot_general(a, b, (((1,), (0,)), ((), ())), preferred_element_type=F32)


def dot_t(a, b):
    return lax.dot_general(a, b, (((1,), (1,)), ((), ())), preferred_element_type=F32)


def split(x):
    high = x.astype(BF16)
    return high, (x - high.astype(F32)).astype(BF16)


def iota(shape, dim):
    return lax.broadcasted_iota(I32, shape, dim)


def codes_of(targets, pairs, signs):
    return targets * 512 + pairs * 2 + (signs > 0).astype(I32)


def stack_halves(first, second):
    pad = jnp.zeros((64 - EXC, 128), I32)
    return jnp.concatenate([first, pad, second, pad], axis=0)


def transposed(codes):
    return jnp.transpose(codes.astype(F32)).astype(I32)


def sign_of(codes, entry):
    return jnp.where((entry & 63) < EXC, ((codes & 1) * 2 - 1).astype(F32), 0.0)


def pair_of(codes):
    return (codes >> 1) & 255


def low_of(codes):
    return (codes >> 9) & 255


def to_bf16(x):
    return x.astype(F32).astype(BF16)


def row_hot(index, width, value=None):
    n = index.shape[1]
    value = jnp.ones((16, n), BF16) if value is None else to_bf16(jnp.broadcast_to(value, (16, n)))
    here = to_bf16(iota((16, n), 0))
    out = []
    for start in range(0, width, 256):
        near = to_bf16(jnp.broadcast_to(index - start, (16, n)))
        out += [jnp.where(here == near - jnp.asarray(s, BF16), value, jnp.zeros((16, n), BF16))
                for s in range(0, min(256, width - start), 16)]
    return jnp.concatenate(out, 0)


def col_hot(index, width, value=None):
    n = index.shape[0]
    value = jnp.ones((n, 128), BF16) if value is None else to_bf16(jnp.broadcast_to(value, (n, 128)))
    here = to_bf16(iota((n, 128), 1))
    out = []
    for start in range(0, width, 256):
        near = to_bf16(jnp.broadcast_to(index - start, (n, 128)))
        out += [jnp.where(here == near - jnp.asarray(s, BF16), value, jnp.zeros((n, 128), BF16))
                for s in range(0, min(256, width - start), 128)]
    return jnp.concatenate(out, 1)


def swap(x):
    return pltpu.roll(x, 64, x.ndim - 1)


def pack_tail(tail):
    return jnp.where(iota((1, 128), 1) < 64, tail[..., 0:8, :], swap(tail[..., 8:16, :]))


def unpack_tail(packed):
    return jnp.concatenate([packed, swap(packed)], axis=-2)


def kernel(
    v_hbm, m_hbm, at_ref, ap_ref, as_ref, bt_ref, bp_ref, bs_ref,
    out_ref,
    v_ref, wide, vp, m_ref, alists, blists, list_sem, mpad, mh, ml,
    ga, gz, za, zsplit,
    acol, arow, a_oh_c, a_oh_r, a_kh, a_kl,
    bcol, brow, b_oh_c, b_oh_r, b_k, fetched, returned, acc,
    ra_out, ra_in, rz_out, rz_in,
    sa_sem, ga_sem, sz_sem, gz_sem, sra_sem, ra_sem, srz_sem, rz_sem,
):
    a, b = lax.axis_index("alpha"), lax.axis_index("beta")

    def alpha_peer(d):
        return lax.rem(a + d, NALPHA)

    def beta_peer(d):
        return lax.rem(b + d, NBETA)

    def alpha_copy(src, dst, send, recv, d):
        return pltpu.make_async_remote_copy(
            src_ref=src, dst_ref=dst, send_sem=send.at[d], recv_sem=recv.at[d],
            device_id=(alpha_peer(d), b), device_id_type=MESH)

    def beta_copy(src, dst, send, recv, d):
        return pltpu.make_async_remote_copy(
            src_ref=src, dst_ref=dst, send_sem=send.at[d], recv_sem=recv.at[d],
            device_id=(a, beta_peer(d)), device_id_type=MESH)

    barrier = pltpu.get_barrier_semaphore()

    @pl.loop(1, NBETA)
    def _(d):
        pl.semaphore_signal(barrier, inc=1, device_id=(a, beta_peer(d)), device_id_type=MESH)

    @pl.loop(1, NALPHA)
    def _(d):
        pl.semaphore_signal(barrier, inc=1, device_id=(alpha_peer(d), b), device_id_type=MESH)

    awin = pl.multiple_of((a // 8) * 128, 128)
    bwin = pl.multiple_of((b // 2) * 384, 128)
    copies = [
        pltpu.make_async_copy(v_hbm, v_ref, list_sem.at[6]),
        pltpu.make_async_copy(m_hbm, m_ref, list_sem.at[7]),
    ]
    for i, ref in enumerate((at_ref, ap_ref, as_ref)):
        copies.append(pltpu.make_async_copy(
            ref.at[:, pl.ds(awin, 128)], alists.at[i], list_sem.at[i]))
    for i, ref in enumerate((bt_ref, bp_ref, bs_ref)):
        copies.append(pltpu.make_async_copy(
            ref.at[:, pl.ds(bwin, 384)], blists.at[i], list_sem.at[3 + i]))
    for copy in copies:
        copy.start()
    for copy in copies:
        copy.wait()

    left_half = iota((1, 128), 1) < 64
    wide[:, 0:COLS] = v_ref[...]
    vp[0:16, :] = wide[:, 0:128]
    vp[16:24, :] = pack_tail(wide[:, 128:256])
    gz[b] = vp[...]
    ga[a] = vp[...]
    mpad[...] = jnp.zeros_like(mpad)
    mpad[0:PAIRS, 0:PAIRS] = m_ref[...]
    high, low = split(mpad[...])
    mh[...] = high
    ml[...] = low

    code = codes_of(blists[0], blists[1], blists[2])
    odd = lax.rem(b, 2) == 1
    first = jnp.where(odd, pltpu.roll(code, 192, 1)[:, :128], code[:, :128])
    second = jnp.where(odd, pltpu.roll(code, 96, 1)[:, :128], pltpu.roll(code, 288, 1)[:, :128])
    code = stack_halves(first, second)
    bcol[...] = code
    brow[...] = transposed(code)

    code = codes_of(alists[0], alists[1], alists[2])
    shift = lax.rem(a, 8) * 16
    first = pltpu.roll(code, lax.rem(128 - shift, 128), 1)
    second = pltpu.roll(code, lax.rem(248 - shift, 128), 1)
    code = stack_halves(first, second)
    acol[...] = code
    arow[...] = transposed(code)

    def beta_step(step):
        rows = brow[pl.ds(pl.multiple_of(step * 8, 8), 8), :]
        cols = pltpu.roll(bcol[...], lax.rem(128 - 8 * step, 128), 1)
        w_c, w_r = [], []
        for k in range(8):
            at = pl.multiple_of(step * 1024 + 128 * k, 128)
            col = cols[:, k:k + 1]
            b_oh_c[pl.ds(at, 128), :] = col_hot(low_of(col), LOW)
            w_c.append(col_hot(pair_of(col), 256, sign_of(col, iota((128, 1), 0))))
            row = rows[k:k + 1, :]
            b_oh_r[:, pl.ds(at, 128)] = row_hot(low_of(row), LOW)
            w_r.append(row_hot(pair_of(row), 256, sign_of(row, iota((1, 128), 1))))
        w_c = jnp.concatenate(w_c, 0)
        uh, ul = dot_t(w_c, mh[...]).astype(BF16), dot_t(w_c, ml[...]).astype(BF16)
        for g in range(4):
            w = jnp.concatenate([w_r[2 * g], w_r[2 * g + 1]], 1)
            kh = dot(uh[256 * g:256 * g + 256], w)
            kl = dot(ul[256 * g:256 * g + 256], w)
            for j in range(4):
                sl = slice(64 * j, 64 * j + 64), slice(128 * (j // 2), 128 * (j // 2) + 128)
                one, two = kh[sl], pltpu.roll(kl[sl], 64, 1)
                mine = left_half if j % 2 == 0 else ~left_half
                b_k[step * 4 + g, 64 * j:64 * j + 64, :] = jnp.where(mine, one, two).astype(BF16)

    same = (iota((256, 256), 0) >> 6) == (iota((256, 256), 1) >> 6)

    def alpha_prepare():
        for g in range(4):
            w_c, w_r = [], []
            for k in (2 * g, 2 * g + 1):
                col, row = acol[:, k:k + 1], arow[k:k + 1, :]
                a_oh_c[128 * k:128 * k + 128, :] = col_hot(col >> 9, NALPHA * ROWS)
                a_oh_r[:, 128 * k:128 * k + 128] = row_hot(row >> 9, NALPHA * ROWS)
                w_c.append(col_hot(pair_of(col), 256, sign_of(col, iota((128, 1), 0))))
                w_r.append(row_hot(pair_of(row), 256, sign_of(row, iota((1, 128), 1))))
            w_c, w_r = jnp.concatenate(w_c, 0), jnp.concatenate(w_r, 1)
            uh, ul = dot(w_c, mh[...]).astype(BF16), dot(w_c, ml[...]).astype(BF16)
            a_kh[g] = jnp.where(same, dot(uh, w_r), 0.0).astype(BF16)
            a_kl[g] = jnp.where(same, dot(ul, w_r), 0.0).astype(BF16)

    pl.loop(0, 4, unroll=4)(beta_step)
    pl.semaphore_wait(barrier, NALPHA + NBETA - 2)

    @pl.loop(1, NBETA)
    def _(d):
        beta_copy(vp, gz.at[b], sz_sem, gz_sem, d).start()

    @pl.loop(1, NALPHA)
    def _(d):
        alpha_copy(vp, ga.at[a], sa_sem, ga_sem, d).start()

    alpha_prepare()
    pl.loop(4, STEPS, unroll=4)(beta_step)

    @pl.loop(1, NALPHA)
    def _(d):
        alpha_copy(vp, ga.at[a], sa_sem, ga_sem, d).wait_recv()

    vh, vl = split(jnp.concatenate(
        [ga[:, 0:16, :].reshape(512, 128), unpack_tail(ga[:, 16:24, :]).reshape(512, 128)], axis=1))
    fh, fl = dot(a_oh_c[...], vh).astype(BF16), dot(a_oh_c[...], vl).astype(BF16)
    rh, rl = [], []
    for g in range(4):
        mine = slice(256 * g, 256 * g + 256)
        high, low = split(
            dot(a_kh[g], fh[mine]) + dot(a_kh[g], fl[mine]) + dot(a_kl[g], fh[mine]))
        rh.append(high)
        rl.append(low)
    rh, rl = jnp.concatenate(rh, 0), jnp.concatenate(rl, 0)
    asum = dot(a_oh_r[...], rh) + dot(a_oh_r[...], rl)
    ra_out[:, 0:16, :] = asum[:, 0:128].reshape(NALPHA, 16, 128)
    ra_out[:, 16:24, :] = pack_tail(asum[:, 128:256].reshape(NALPHA, 16, 128))

    @pl.loop(1, NALPHA)
    def _(d):
        alpha_copy(ra_out.at[alpha_peer(d)], ra_in.at[a], sra_sem, ra_sem, d).start()

    @pl.loop(1, NBETA)
    def _(d):
        beta_copy(vp, gz.at[b], sz_sem, gz_sem, d).wait_recv()

    for m in range(NBETA // 2):
        first, second = gz[2 * m], gz[2 * m + 1]
        turned = swap(second[0:16])
        za[:, 384 * m:384 * m + 128] = first[0:16]
        za[:, 384 * m + 128:384 * m + 256] = jnp.where(left_half, unpack_tail(first[16:24]), turned)
        za[:, 384 * m + 256:384 * m + 384] = jnp.where(
            left_half, turned, swap(unpack_tail(second[16:24])))
    for h in range(HIGH):
        high, low = split(za[:, LOW * h:LOW * (h + 1)])
        zsplit[32 * h:32 * h + 16, :] = high
        zsplit[32 * h + 16:32 * h + 32, :] = low
    acc[...] = jnp.zeros_like(acc)

    quarter = iota((1, 256), 1) >> 6

    def high_rows(step):
        return brow[pl.ds(pl.multiple_of(step * 8, 8), 8), :] >> 17

    def pair_row(rows, g):
        return jnp.concatenate([rows[2 * g:2 * g + 1, :], rows[2 * g + 1:2 * g + 2, :]], axis=1)

    @pl.loop(0, STEPS, unroll=3)
    def _(step):
        highs = high_rows(step)
        for g in range(4):
            at = pl.multiple_of(step * 1024 + 256 * g, 256)
            picked = dot(zsplit[...], b_oh_r[:, pl.ds(at, 256)])
            hrow = pair_row(highs, g)
            f = picked[0:32]
            for h in range(1, HIGH):
                f = jnp.where(hrow == h, picked[32 * h:32 * h + 32], f)
            fetched[:, pl.ds(at, 256)] = f.astype(BF16)

    @pl.loop(0, STEPS, unroll=3)
    def _(step):
        for g in range(4):
            at = pl.multiple_of(step * 1024 + 256 * g, 256)
            f = fetched[:, pl.ds(at, 256)].astype(F32)
            lhs = jnp.concatenate(
                [jnp.where(quarter == j, f, 0.0).astype(BF16) for j in range(4)], axis=0)
            back = dot(lhs, b_k[step * 4 + g])
            parts = []
            for j in (0, 2):
                h0, l0 = back[32 * j:32 * j + 16], back[32 * j + 16:32 * j + 32]
                h1, l1 = back[32 * j + 32:32 * j + 48], back[32 * j + 48:32 * j + 64]
                parts.append(jnp.where(left_half, h0 + l0, h1 + l1)
                             + pltpu.roll(jnp.where(left_half, h1, h0), 64, 1))
            r = jnp.concatenate(parts, 1)
            high, low = split(r)
            returned[0:16, pl.ds(at, 256)] = high
            returned[16:32, pl.ds(at, 256)] = low

    @pl.loop(0, STEPS, unroll=3)
    def _(step):
        highs = high_rows(step)
        lhs = []
        for g in range(4):
            at = pl.multiple_of(step * 1024 + 256 * g, 256)
            r = returned[:, pl.ds(at, 256)].astype(F32)
            hrow = pair_row(highs, g)
            lhs.append(jnp.concatenate(
                [jnp.where(hrow == h, r, 0.0).astype(BF16) for h in range(HIGH)], axis=0))
        at = pl.multiple_of(step * 1024, 1024)
        acc[...] += dot(jnp.concatenate(lhs, 1), b_oh_c[pl.ds(at, 1024), :])

    for h in range(HIGH):
        za[:, LOW * h:LOW * (h + 1)] = acc[32 * h:32 * h + 16, :] + acc[32 * h + 16:32 * h + 32, :]
    for m in range(NBETA // 2):
        t0 = za[:, 384 * m:384 * m + 128]
        t1 = za[:, 384 * m + 128:384 * m + 256]
        t2 = za[:, 384 * m + 256:384 * m + 384]
        rz_out[2 * m, 0:16] = t0
        rz_out[2 * m, 16:24] = pack_tail(t1)
        rz_out[2 * m + 1, 0:16] = swap(jnp.where(left_half, t2, t1))
        rz_out[2 * m + 1, 16:24] = pack_tail(swap(t2))

    @pl.loop(1, NBETA)
    def _(d):
        beta_copy(rz_out.at[beta_peer(d)], rz_in.at[b], srz_sem, rz_sem, d).start()

    ra_in[a] = ra_out[a]
    rz_in[b] = rz_out[b]

    @pl.loop(1, NALPHA)
    def _(d):
        alpha_copy(vp, ga.at[a], sa_sem, ga_sem, d).wait_send()
        alpha_copy(ra_out.at[alpha_peer(d)], ra_in.at[a], sra_sem, ra_sem, d).wait()

    total = ra_in[0]
    for i in range(1, NALPHA):
        total = total + ra_in[i]

    @pl.loop(1, NBETA)
    def _(d):
        beta_copy(vp, gz.at[b], sz_sem, gz_sem, d).wait_send()
        beta_copy(rz_out.at[beta_peer(d)], rz_in.at[b], srz_sem, rz_sem, d).wait()

    for i in range(NBETA):
        total = total + rz_in[i]
    out_ref[:, 0:128] = total[0:16]
    out_ref[:, 128:COLS] = unpack_tail(total[16:24])[:, 0:COLS - 128]


def local(vector, integrals, *lists):
    vmem = pl.BlockSpec(memory_space=pltpu.VMEM)
    hbm = pl.BlockSpec(memory_space=pltpu.HBM)
    dma = pltpu.SemaphoreType.DMA

    def block(*shape):
        return pltpu.VMEM(shape, F32)

    return pl.pallas_call(
        kernel,
        out_shape=jax.ShapeDtypeStruct((ROWS, COLS), F32),
        in_specs=[hbm] * 8,
        out_specs=vmem,
        scratch_shapes=[
            block(ROWS, COLS),
            block(ROWS, 256),
            block(24, 128),
            block(PAIRS, PAIRS),
            pltpu.VMEM((3, EXC, 128), I32),
            pltpu.VMEM((3, EXC, 384), I32),
            dma((8,)),
            block(256, 256),
            pltpu.VMEM((256, 256), BF16),
            pltpu.VMEM((256, 256), BF16),
            block(NALPHA, 24, 128),
            block(NBETA, 24, 128),
            block(ROWS, NBETA * COLS),
            pltpu.VMEM((2 * HIGH * ROWS, LOW), BF16),
            pltpu.VMEM((128, 128), I32),
            pltpu.VMEM((128, 128), I32),
            pltpu.VMEM((1024, NALPHA * ROWS), BF16),
            pltpu.VMEM((NALPHA * ROWS, 1024), BF16),
            pltpu.VMEM((4, 256, 256), BF16),
            pltpu.VMEM((4, 256, 256), BF16),
            pltpu.VMEM((128, 128), I32),
            pltpu.VMEM((128, 128), I32),
            pltpu.VMEM((ENTRIES, LOW), BF16),
            pltpu.VMEM((LOW, ENTRIES), BF16),
            pltpu.VMEM((TILES, 256, 128), BF16),
            pltpu.VMEM((2 * ROWS, ENTRIES), BF16),
            pltpu.VMEM((2 * ROWS, ENTRIES), BF16),
            block(2 * HIGH * ROWS, LOW),
            block(NALPHA, 24, 128),
            block(NALPHA, 24, 128),
            block(NBETA, 24, 128),
            block(NBETA, 24, 128),
            dma((NALPHA,)), dma((NALPHA,)), dma((NBETA,)), dma((NBETA,)),
            dma((NALPHA,)), dma((NALPHA,)), dma((NBETA,)), dma((NBETA,)),
        ],
        compiler_params=pltpu.CompilerParams(
            collective_id=0, has_side_effects=True, vmem_limit_bytes=54 * 1024 * 1024),
    )(vector, integrals, *lists)


def solution(mesh):
    placed = (P("alpha", "beta"), P(), P(), P(), P(), P(), P(), P())
    return jax.shard_map(
        local, mesh=mesh, in_specs=placed, out_specs=P("alpha", "beta"), check_vma=False
    )
```

time: 68.5 us -> 55.1 us (0.80)
  the two profiles are of different devices: /device:TPU:2 before, /device:TPU:1 now
where the time goes in v3:
time: 55.1 us; the launch traced here: 54.8 us
  Pallas kernels  53.5 us (97%)
  local copies, waits for them, and re-layouts  1.32 us (2%)
    pallas_call x1, Pallas kernels, local(): pl.pallas_call(kernel, out_shape=jax.ShapeDtypeStruct((ROWS, COLS), F32),...  53.5 us
    unnamed x1, local copies, waits for them, and re-layouts  1.32 us

profile of v3, /device:TPU:1, one launch (start us, length us, event | category | flops | bytes accessed | tf_op | source)
XLA Modules:
  0.0 54.8 jit_solution(1725487942510216696)
XLA Ops:
  0.0 53.5 %shard_map.82 = f32[16,192]{1,0:T(8,128)} custom-call(f32[16,192]{1,0:T(8,128)} %v_hbm.1, f32[196,196]{1,0:T(8,128)} %m_hbm.1, s32[56,512]{1,0:T(8,128)} %at_ref.1, s32[56,512]{1,0:T(8,128)} %ap_ref.1, s32[56,512]{1,0:T(8,128)} %as_ref.1, s32[56,3072]{1,0:T(8,128)} %bt_ref.1, s32[56,3072]{1,0:T(8,128)} %bp_ref.1, s32[56,3072]{1,0:T(8,128)} %bs_ref.1), custom_call_target="tpu_custom_call" | custom-call | tf_op jit(solution)/shard_map/pallas_call | solution.py:377
  53.5 1.3 %copy.10 = f32[16,192]{1,0:T(8,128)} copy(f32[16,192]{1,0:T(8,128)} %shard_map.82) | data formatting | bytes 24576

commit v4 on v3

--- a/solution.py
+++ b/solution.py
@@ -284,7 +284,7 @@
     def pair_row(rows, g):
         return jnp.concatenate([rows[2 * g:2 * g + 1, :], rows[2 * g + 1:2 * g + 2, :]], axis=1)
 
-    @pl.loop(0, STEPS, unroll=3)
+    @pl.loop(0, STEPS, unroll=6)
     def _(step):
         highs = high_rows(step)
         for g in range(4):
@@ -296,7 +296,7 @@
                 f = jnp.where(hrow == h, picked[32 * h:32 * h + 32], f)
             fetched[:, pl.ds(at, 256)] = f.astype(BF16)
 
-    @pl.loop(0, STEPS, unroll=3)
+    @pl.loop(0, STEPS, unroll=6)
     def _(step):
         for g in range(4):
             at = pl.multiple_of(step * 1024 + 256 * g, 256)
@@ -315,7 +315,7 @@
             returned[0:16, pl.ds(at, 256)] = high
             returned[16:32, pl.ds(at, 256)] = low
 
-    @pl.loop(0, STEPS, unroll=3)
+    @pl.loop(0, STEPS, unroll=6)
     def _(step):
         highs = high_rows(step)
         lhs = []

time: 55.1 us -> 54 us (0.980)
  Pallas kernels: 53.5 us -> 52.4 us
    pallas_call x1, Pallas kernels: 53.5 us -> 52.4 us  [local(): pl.pallas_call(kernel, out_shape=jax.ShapeDtypeStruct((ROWS, COLS), F32),...]
where the time goes in v4:
time: 54 us; the launch traced here: 53.7 us
  Pallas kernels  52.4 us (97%)
  local copies, waits for them, and re-layouts  1.32 us (2%)
    pallas_call x1, Pallas kernels, local(): pl.pallas_call(kernel, out_shape=jax.ShapeDtypeStruct((ROWS, COLS), F32),...  52.4 us
    unnamed x1, local copies, waits for them, and re-layouts  1.32 us

profile of v4, /device:TPU:1, one launch (start us, length us, event | category | flops | bytes accessed | tf_op | source)
XLA Modules:
  0.0 53.7 jit_solution(12633198604884433836)
XLA Ops:
  0.0 52.4 %shard_map.82 = f32[16,192]{1,0:T(8,128)} custom-call(f32[16,192]{1,0:T(8,128)} %v_hbm.1, f32[196,196]{1,0:T(8,128)} %m_hbm.1, s32[56,512]{1,0:T(8,128)} %at_ref.1, s32[56,512]{1,0:T(8,128)} %ap_ref.1, s32[56,512]{1,0:T(8,128)} %as_ref.1, s32[56,3072]{1,0:T(8,128)} %bt_ref.1, s32[56,3072]{1,0:T(8,128)} %bp_ref.1, s32[56,3072]{1,0:T(8,128)} %bs_ref.1), custom_call_target="tpu_custom_call" | custom-call | tf_op jit(solution)/shard_map/pallas_call | solution.py:377
  52.4 1.3 %copy.10 = f32[16,192]{1,0:T(8,128)} copy(f32[16,192]{1,0:T(8,128)} %shard_map.82) | data formatting | bytes 24576
